TPU v7x, 32 devices: a whole 2x2x4 slice. The times are simulated.
32 devices in a mesh: row: 8 (over y, x, core), col: 4 (over z).
Axes of the slice: x: 2, y: 2, z: 4, core: 2. Of those that a mesh axis runs over, the one named last changes fastest.
Arguments:
- ancestor_inverse: bfloat16 [2048, 2048], P('row', 'col'), may hold values from -6 to 6
- panel_one: bfloat16 [2048, 512], P(('row', 'col')), may hold values from -0.125 to 0.125
- ancestors_one: int32 [2, 7], replicated, may hold values from 0 to 7, as said below
- diag_inverse_one: bfloat16 [2, 256, 256], replicated, may hold values from -6 to 6
- panel_two: bfloat16 [2048, 512], P(('row', 'col')), may hold values from -0.125 to 0.125
- link_two: bfloat16 [2, 256, 256], replicated, may hold values from -0.375 to 0.375
- ancestors_two: int32 [2, 6], replicated, may hold values from 0 to 7, as said below
- diag_inverse_two: bfloat16 [2, 256, 256], replicated, may hold values from -6 to 6
- widths: int32 [4], replicated, may hold values from 128 to 256, as said below
Outputs:
- column_one: bfloat16 [2048, 512], P(('row', 'col'))
- block_one: bfloat16 [2, 256, 256], replicated
- column_two: bfloat16 [2048, 512], P(('row', 'col'))
- parent_rows_two: bfloat16 [2, 256, 256], replicated
- block_two: bfloat16 [2, 256, 256], replicated
Inputs may be any that keep to these rules, and one draw needn't show every extreme that they name: `ancestors_one`: each row lists 7 distinct tiles in ascending order; 0 and 7 are always among them. `ancestors_two`: row s lists 6 distinct entries of row s of ancestors_one in ascending order; 0 and 7 are always among them. `widths`: at least one supernode uses all 256 columns.
All inputs are finite; a program needn't handle non-finite values.
Results may differ from a plain program's by a relative error of at most 0.0055.
Values may be sent and summed in bfloat16 or wider, within the bound.
A program may use at most 64 MiB of HBM per device.

v0:
```python
import jax
import jax.numpy as jnp
from jax import lax
from jax.sharding import PartitionSpec as P


def from_root(value, axis, source):
    kept = jnp.where(lax.axis_index(axis) == source, value, 0).astype(value.dtype)
    return lax.psum(kept, axis)


def tile_members(ancestors, first_row, row_count, tile_width):
    row_ids = first_row + jnp.arange(row_count, dtype=jnp.int32)
    tile_of_row = row_ids // tile_width
    matches = (ancestors[:, None, :] == tile_of_row[None, :, None]).astype(jnp.int32)
    return jnp.sum(matches, axis=2).astype(jnp.bfloat16)


def row_mask(members, keep_pair, tile_width):
    combined = members.T[:, :, None] * keep_pair[None, :, :]
    return combined.reshape(members.shape[1], 2 * tile_width)


def columns_joint(share_block):
    whole_rows = lax.all_gather(share_block, "col", axis=0, tiled=True)
    per_group = lax.axis_size("row") // lax.axis_size("col")
    first_root = lax.axis_index("col") * per_group
    pieces = []
    for offset in range(per_group):
        pieces.append(from_root(whole_rows, "row", first_root + offset))
    return jnp.concatenate(pieces, axis=0)


def product_joint(ancestor_inverse, lower_columns):
    return lax.psum_scatter(
        jnp.dot(ancestor_inverse, lower_columns, preferred_element_type=jnp.float32),
        "col",
        scatter_dimension=0,
        tiled=True,
    )


def local(
    ancestor_inverse,
    panel_one,
    ancestors_one,
    diag_inverse_one,
    panel_two,
    link_two,
    ancestors_two,
    diag_inverse_two,
    widths,
):
    tile_width = diag_inverse_one.shape[-1]
    local_rows = ancestor_inverse.shape[0]
    share_rows = panel_one.shape[0]
    share_start = lax.axis_index("row") * local_rows + lax.axis_index("col") * share_rows
    columns = jnp.arange(tile_width, dtype=jnp.int32)
    keep_columns = (columns[None, :] < widths[:, None]).astype(jnp.bfloat16)
    member_one = tile_members(ancestors_one, share_start, share_rows, tile_width)
    member_two = tile_members(ancestors_two, share_start, share_rows, tile_width)
    lower_one = panel_one * row_mask(member_one, keep_columns[0:2], tile_width)
    lower_two = panel_two * row_mask(member_two, keep_columns[2:4], tile_width)
    split_one = lower_one.reshape(share_rows, 2, tile_width)
    split_two = lower_two.reshape(share_rows, 2, tile_width)
    keep_parent = keep_columns[0:2]
    keep_child = keep_columns[2:4]
    pivot_one = diag_inverse_one.astype(jnp.float32) * (
        keep_parent[:, :, None] * keep_parent[:, None, :]
    ).astype(jnp.float32)
    pivot_two = diag_inverse_two.astype(jnp.float32) * (
        keep_child[:, :, None] * keep_child[:, None, :]
    ).astype(jnp.float32)
    link_masked = link_two * keep_parent[:, :, None] * keep_child[:, None, :]
    both_columns = columns_joint(jnp.concatenate([lower_one, lower_two], axis=1))
    product_all = product_joint(ancestor_inverse, both_columns)
    product_one = product_all[:, : 2 * tile_width]
    product_rest = product_all[:, 2 * tile_width :]
    view_one = product_one.reshape(share_rows, 2, tile_width)
    column_one = (-(view_one * member_one.T[:, :, None].astype(jnp.float32))).astype(jnp.bfloat16)
    diag_part = jnp.einsum(
        "isa,isb->sab", split_one, column_one, preferred_element_type=jnp.float32
    )
    diag_total = lax.psum(diag_part, ("row", "col"))
    block_one = (pivot_one - diag_total).astype(jnp.bfloat16)
    cross_part = jnp.einsum(
        "isa,isb->sab", column_one, split_two, preferred_element_type=jnp.float32
    )
    cross_total = lax.psum(cross_part, ("row", "col"))
    view_two = product_rest.reshape(share_rows, 2, tile_width)
    second_total = view_two + jnp.einsum(
        "isa,sab->isb", column_one, link_masked, preferred_element_type=jnp.float32
    )
    column_two = (-(second_total * member_two.T[:, :, None].astype(jnp.float32))).astype(
        jnp.bfloat16
    )
    lower_part = jnp.einsum(
        "isa,isb->sab", split_two, column_two, preferred_element_type=jnp.float32
    )
    lower_total = lax.psum(lower_part, ("row", "col"))
    parent_block = (
        -(
            jnp.einsum("sab,sbc->sac", block_one, link_masked, preferred_element_type=jnp.float32)
            + cross_total
        )
    ).astype(jnp.bfloat16)
    block_two = (
        pivot_two
        - jnp.einsum("sba,sbc->sac", link_masked, parent_block, preferred_element_type=jnp.float32)
        - lower_total
    ).astype(jnp.bfloat16)
    return (
        column_one.reshape(share_rows, 2 * tile_width),
        block_one,
        column_two.reshape(share_rows, 2 * tile_width),
        parent_block,
        block_two,
    )


def solution(mesh):
    in_specs = (
        P("row", "col"),
        P(("row", "col"), None),
        P(),
        P(),
        P(("row", "col"), None),
        P(),
        P(),
        P(),
        P(),
    )
    out_specs = (P(("row", "col"), None), P(), P(("row", "col"), None), P(), P())
    return jax.shard_map(local, mesh=mesh, in_specs=in_specs, out_specs=out_specs, check_vma=False)
```

profile of v0, /device:TPU:1, one launch (start us, length us, event | category | flops | bytes accessed | tf_op | source)
XLA Modules:
  0.0 263.8 jit_solution(16490464086178786382)
XLA Ops:
  7.2 0.0 copy-start
  7.2 0.0 all-reduce.7.cloned.1.call-start
  7.3 0.7 fusion.30
  8.0 0.8 copy.57
  8.8 0.1 fusion.28
  8.9 0.8 copy.59
  9.6 0.1 fusion.29
  9.7 0.1 copy.58
  9.9 0.1 copy.60
  10.0 0.1 mul.125
  10.1 0.1 mul.119
  10.3 0.9 multiply_multiply_fusion.4
  11.2 15.3 %all_gather.3 = bf16[256,1024]{1,0:T(8,128)(2,1)S(1)} all-gather(bf16[64,1024]{1,0:T(8,128)(2,1)S(1)} %pad_maximum_fusion), channel_id=1, replica_groups=mesh['row'=8,'col'=4] {'col'}, dimensions={0}, use_global_device_ids=true | all-gather | bytes 655360 | tf_op jit(solution)/shard_map/all_gather | solution.py:25
  26.5 1.1 broadcast_select_fusion.1
  27.6 0.0 all-reduce.7.cloned.1.call-update
  27.6 0.0 reduce-scatter.4.cloned.1.call-start
  27.6 59.0 %all-reduce.7.cloned.1.call-done = (bf16[256,1024]{1,0:T(8,128)(2,1)}, bf16[256,1024]{1,0:T(8,128)(2,1)}) async-done(((bf16[256,1024]{1,0:T(8,128)(2,1)}, bf16[256,1024]{1,0:T(8,128)(2,1)}), (bf16[256,1024]{1,0:T(8,128)(2,1)}, bf16[256,1024]{1,0:T(8,128)(2,1)})) %all-reduce.7.cloned.1.call-update) | async-done | bytes 1048592 | tf_op jit(solution)/shard_map/psum | solution.py:9
  86.6 0.0 copy-done
  86.6 1.7 convolution_bitcast_fusion
  88.3 1.3 copy.74
  89.6 0.0 reduce-scatter.4.cloned.1.call-update
  89.6 0.0 all-reduce.5.cloned.1.call-start
  89.7 27.2 %reduce-scatter.4.cloned.1.call-done = f32[64,1024]{1,0:T(8,128)} async-done(((f32[256,1024]{1,0:T(8,128)}), f32[64,1024]{1,0:T(8,128)}) %reduce-scatter.4.cloned.1.call-update) | async-done | bytes 262160
  116.8 1.0 fusion.34
  117.8 0.1 copy.77
  118.0 0.1 copy.65
  118.1 0.1 copy.76
  118.2 0.0 copy-start.1
  118.2 0.1 copy.62
  118.4 0.1 negate_convert_fusion
  118.4 1.1 fusion.23
  119.5 1.1 fusion.21
  120.6 0.0 copy-done.1
  120.6 0.3 fusion.7
  120.9 1.1 fusion.19
  122.0 0.0 copy-start.6
  122.0 0.0 all-reduce.5.cloned.1.call-update
  122.0 0.7 copy.70
  122.8 0.6 copy.81
  123.4 131.0 %all-reduce.5.cloned.1.call-done = (f32[2,256,256]{2,1,0:T(8,128)}, f32[2,256,256]{2,1,0:T(8,128)}, f32[2,256,256]{2,1,0:T(8,128)}) async-done(((f32[2,256,256]{2,1,0:T(8,128)}, f32[2,256,256]{2,1,0:T(8,128)}, f32[2,256,256]{2,1,0:T(8,128)}), (f32[2,256,256]{2,1,0:T(8,128)}, f32[2,256,256]{2,1,0:T(8,128)}, f32[2,256,256]{2,1,0:T(8,128)})) %all-reduce.5.cloned.1.call-update) | async-done | bytes 1572880 | tf_op jit(solution)/shard_map/psum | solution.py:84
  254.4 0.0 copy-start.4
  254.4 0.0 copy-done.6
  254.5 0.0 copy-start.5
  254.5 0.0 copy-start.7
  254.5 1.3 subtract_convert_fusion
  255.8 0.0 copy-start.2
  255.8 0.0 copy-done.4
  255.8 0.3 fusion.3
  256.1 0.0 copy-start.3
  256.1 0.0 copy-done.5
  256.1 0.0 copy-done.7
  256.2 1.1 fusion.2
  257.3 0.0 copy-done.2
  257.3 0.0 copy-done.3
  (10 shorter events, 0.1 us)
Async XLA Ops:
  7.2 79.4 %copy-start = (bf16[256,512]{1,0:T(8,128)(2,1)S(1)}, bf16[256,512]{1,0:T(8,128)(2,1)}, u32[]{:S(2)}) copy-start(bf16[256,512]{1,0:T(8,128)(2,1)} %param.9) | copy-start | bytes 786436
  7.2 79.4 %all-reduce.7.cloned.1.call-start = ((), (), s32[]{:S(2)}) async-start(), calls=%async_computation.3 | async-start | bytes 2097152 | tf_op jit(solution)/shard_map/psum | solution.py:9
  27.6 89.3 %reduce-scatter.4.cloned.1.call-start = ((), (), s32[]{:S(2)}) async-start(), calls=%async_computation.1 | async-start | bytes 1310720
  89.6 164.8 %all-reduce.5.cloned.1.call-start = ((), (), s32[]{:S(2)}) async-start(), calls=%async_computation.2 | async-start | bytes 3145728 | tf_op jit(solution)/shard_map/psum | solution.py:84
  118.2 2.4 copy-start.1
  122.0 132.5 %copy-start.6 = (bf16[2,256,256]{2,1,0:T(8,128)(2,1)S(1)}, bf16[2,256,256]{2,1,0:T(8,128)(2,1)}, u32[]{:S(2)}) copy-start(bf16[2,256,256]{2,1,0:T(8,128)(2,1)} %param.12) | copy-start | bytes 786436
  254.4 1.3 copy-start.4
  254.5 1.7 copy-start.5
  254.5 1.7 copy-start.7
  255.8 1.5 copy-start.2
  256.1 1.2 copy-start.3
Sparse Core Ops, SparseCore 0:
  27.7 58.8 all-reduce.6
  89.8 27.0 reduce-scatter.3
  123.4 130.9 all-reduce.4
where the time goes:
time: 266 us; the launch traced here: 264 us
  waiting for transfers between devices  217 us (82%)
  blocking collectives  15.3 us (6%)
  between operations  14 us (5%)
  matrix products  6.66 us (3%)
  local copies, waits for them, and re-layouts  6.24 us (2%)
  other arithmetic  4.32 us (2%)
    psum x1, waiting for transfers between devices, local(): diag_total = lax.psum(diag_part, ('row', 'col'))  131 us
    psum x1, waiting for transfers between devices, from_root(): return lax.psum(kept, axis)  59 us
    unnamed x4, waiting for transfers between devices  27.2 us
    all_gather x1, blocking collectives, columns_joint(): whole_rows = lax.all_gather(share_block, 'col', axis=0, tiled=True)  15.3 us
  transfers between devices with their start and end apart: 3, of which 3 were waited for; matrix products, arithmetic and copies ran while one was open for 1% of the time, Pallas kernels for 0%

commit v1 on v0

v1 whole, which is shorter than its diff:
```python
import functools

import jax
import jax.numpy as jnp
from jax import lax
from jax.experimental import pallas as pl
from jax.experimental.pallas import tpu as pltpu
from jax.sharding import PartitionSpec as P

MESH = pl.DeviceIdType.MESH
PIECES = 4
F32 = jnp.float32
BF16 = jnp.bfloat16


def left_t(a, b):
    return lax.dot_general(a, b, (((0,), (0,)), ((), ())), preferred_element_type=F32)


def kernel(
    n,
    depth,
    panel_one,
    panel_two,
    anc_one,
    anc_two,
    widths,
    inv_hbm,
    diag_one_hbm,
    diag_two_hbm,
    link_hbm,
    col_one_out,
    block_one_out,
    col_two_out,
    parent_out,
    block_two_out,
    inv,
    diag_one,
    diag_two,
    link,
    lines,
    relay,
    panels,
    prod,
    prod_send,
    prod_recv,
    pair_send,
    pair_recv,
    sums,
    plane_send,
    plane_recv,
    part,
    line_send,
    line_recv,
    whole,
    load_sem,
    a_sem,
    b_sem,
    c_send,
    c_recv,
    f_send,
    f_recv,
    l_sem,
    p_sem,
    pair_sem,
    ps_sem,
    ls_sem,
    lg_sem,
    pg_sem,
    fg_sem,
):
    width = diag_one.shape[-1]
    share = panel_one.shape[0]
    small = n == PIECES
    row = lax.axis_index("row")
    z = lax.axis_index("col")
    chip = row // 2
    core = row % 2
    mine = chip % PIECES
    group = chip - mine
    z_group = z - z % PIECES
    sibling = (2 * chip + (1 - core), z)

    def on_chip(c):
        return (2 * c + core, z)

    def on_line(level):
        return (row, level)

    def send(src, dst, ssem, rsem, target):
        copy = pltpu.make_async_remote_copy(
            src_ref=src, dst_ref=dst, send_sem=ssem, recv_sem=rsem, device_id=target, device_id_type=MESH
        )
        copy.start()
        return copy

    def arrived(dst, rsem):
        pltpu.make_async_copy(dst, dst, rsem).wait()

    loads = []
    for i, (src, dst) in enumerate(
        ((inv_hbm, inv), (link_hbm, link), (diag_one_hbm, diag_one), (diag_two_hbm, diag_two))
    ):
        loads.append(pltpu.make_async_copy(src, dst, load_sem.at[i]))
        loads[-1].start()

    barrier = pltpu.get_barrier_semaphore()
    pl.semaphore_signal(barrier, inc=1, device_id=sibling, device_id_type=MESH)
    for i in range(1, n):
        pl.semaphore_signal(barrier, inc=1, device_id=on_chip((chip + i) % n), device_id_type=MESH)
    for i in range(1, depth):
        pl.semaphore_signal(barrier, inc=1, device_id=on_line((z + i) % depth), device_id_type=MESH)

    columns = lax.broadcasted_iota(jnp.int32, (share, width), 1)
    member = []
    for p in range(PIECES):
        ancestors, s = (anc_one, p) if p < 2 else (anc_two, p - 2)
        found = jnp.int32(0)
        for t in range(ancestors.shape[1]):
            found += jnp.where(ancestors[s, t] == row, 1, 0).astype(jnp.int32)
        member.append(found.astype(F32))
        source = panel_one if p < 2 else panel_two
        values = source[:, s * width : (s + 1) * width]
        kept = jnp.where(columns < widths[p] * found, values.astype(F32), 0.0).astype(BF16)
        lines[z, p] = kept
    relay[mine] = lines[z, mine]

    pl.semaphore_wait(barrier, 1 + (n - 1) + (depth - 1))

    sent = []
    copies = []
    for i in range(1, PIECES):
        p = (mine + i) % PIECES
        copies.append(
            send(lines.at[z, p], relay.at[mine], a_sem.at[0, i], a_sem.at[1, i], on_chip(group + p))
        )
    for copy in copies:
        copy.wait_recv()
    sent += copies
    is_relay = group == z_group

    def local_piece():
        panels[mine, core, z] = relay[z % PIECES]

    if small:
        local_piece()
        first = None
    else:
        first = pltpu.make_async_remote_copy(
            src_ref=relay.at[z % PIECES],
            dst_ref=panels.at[mine, core, z],
            send_sem=b_sem.at[0, 0],
            recv_sem=b_sem.at[1, z],
            device_id=on_line(group + z % PIECES),
            device_id_type=MESH,
        )
        pl.when(is_relay)(local_piece)
        pl.when(jnp.logical_not(is_relay))(first.start)
    for i in range(1, PIECES):
        j = (z + i) % PIECES
        sent.append(
            send(relay.at[j], panels.at[mine, core, z], b_sem.at[0, i], b_sem.at[1, z], on_line(group + j))
        )
    line_copies = []

    def share_line():
        for i in range(1, depth):
            line_copies.append(
                send(lines.at[z], lines.at[z], l_sem.at[0, i], l_sem.at[1, z], on_line((z + i) % depth))
            )

    chunks = [(z + i) % depth for i in range(depth)] if small else [None]

    def chunk(p, c, level):
        return panels.at[p, c] if level is None else panels.at[p, c, level]

    def slot(level):
        return 0 if level is None else level

    def spread(start):
        for t, level in enumerate(chunks):
            if start:
                if level is None:
                    for i in range(1, depth):
                        other = (z + i) % depth
                        arrived(panels.at[mine, core, other], b_sem.at[1, other])
                elif t > 0:
                    arrived(panels.at[mine, core, level], b_sem.at[1, level])
            here = chunk(mine, core, level)
            targets = [(on_chip((chip + i) % n), c_recv) for i in range(1, n)] + [(sibling, f_recv)]
            for i, (target, rsem) in enumerate(targets):
                copy = pltpu.make_async_remote_copy(
                    src_ref=here,
                    dst_ref=here,
                    send_sem=c_send.at[t, i],
                    recv_sem=rsem.at[mine, slot(level)],
                    device_id=target,
                    device_id_type=MESH,
                )
                if start:
                    copy.start()
                else:
                    copy.wait_send()
            if start and small and t == 0:
                share_line()

    if small:
        spread(True)
    else:
        share_line()
        pl.when(is_relay)(functools.partial(spread, True))

    def forward(p, start):
        for t, level in enumerate(chunks):
            here = chunk(p, core, level)
            if start:
                arrived(here, c_recv.at[p, slot(level)])
            copy = pltpu.make_async_remote_copy(
                src_ref=here,
                dst_ref=here,
                send_sem=f_send.at[p, t],
                recv_sem=f_recv.at[p, slot(level)],
                device_id=sibling,
                device_id_type=MESH,
            )
            if start:
                copy.start()
            else:
                copy.wait_send()

    if not small:
        pl.when(jnp.logical_not(is_relay))(functools.partial(forward, mine, True))
    if small:
        for t, level in enumerate(chunks):
            for i in range(1, PIECES):
                p = (mine + i) % PIECES
                here = chunk(p, core, level)
                arrived(here, c_recv.at[p, level])
                sent.append(send(here, here, f_send.at[p, t], f_recv.at[p, level], sibling))
    else:
        for i in range(1, PIECES):
            forward((mine + i) % PIECES, True)
    for copy in loads:
        copy.wait()
    for p in range(PIECES):
        for level in range(depth if small else 1):
            arrived(chunk(p, 1 - core, level if small else None), f_recv.at[p, level])

    for p in range(PIECES):
        stacked = panels[p].reshape(2 * depth * share, width)
        product = jnp.dot(inv[...], stacked, preferred_element_type=F32) * member[p]
        prod[p] = product
        prod_send[:, p] = product.astype(BF16).reshape(depth, share, width)
    for i in range(1, depth):
        other = (z + i) % depth
        sent.append(
            send(prod_send.at[other], prod_recv.at[z], p_sem.at[0, i], p_sem.at[1, z], on_line(other))
        )
    for i in range(1, depth):
        other = (z + i) % depth
        arrived(lines.at[other], l_sem.at[1, other])

    def square(ref, p):
        return ref[:, p].reshape(depth * share, width)

    def inner(s):
        first_lower, second_lower = square(lines, s), square(lines, 2 + s)
        first, second = square(prod_send, s), square(prod_send, 2 + s)
        return left_t(first_lower, first), left_t(second_lower, first), left_t(second_lower, second)

    for m, value in enumerate(inner(1 - core)):
        pair_send[m] = value.astype(BF16)
    pair = send(pair_send, pair_recv, pair_sem.at[0], pair_sem.at[1], sibling)
    sent.append(pair)
    for m, value in enumerate(inner(core)):
        sums[m] = value
    pair.wait_recv()

    rows = width // n
    for m in range(3):
        value = sums[m] + pair_recv[m].astype(F32)
        sums[m] = value
        plane_send[:, m] = value.astype(BF16).reshape(n, rows, width)
    for i in range(1, n):
        other = (chip + i) % n
        sent.append(
            send(plane_send.at[other], plane_recv.at[chip], ps_sem.at[0, i], ps_sem.at[1, chip], on_chip(other))
        )
    first_row = pl.multiple_of(chip * rows, rows)
    for i in range(1, n):
        other = (chip + i) % n
        arrived(plane_recv.at[other], ps_sem.at[1, other])
    for m in range(3):
        value = sums[m, pl.ds(first_row, rows)]
        for i in range(1, n):
            value += plane_recv[(chip + i) % n, m].astype(F32)
        part[m] = value

    owners = line_send.shape[0]
    owned = rows // owners
    for m in range(3):
        line_send[:, m] = part[m].astype(BF16).reshape(owners, owned, width)
    every = owners == depth

    def line_part(copy_at, start):
        if every:
            return
        for t in range(owners):
            copy = copy_at(t, t)

            @pl.when(z != t)
            def _():
                if start:
                    copy.start()
                else:
                    copy.wait_send()

    def reduce_copy(t, i):
        return pltpu.make_async_remote_copy(
            src_ref=line_send.at[t],
            dst_ref=line_recv.at[z],
            send_sem=ls_sem.at[0, i],
            recv_sem=ls_sem.at[1, z],
            device_id=on_line(t),
            device_id_type=MESH,
        )

    if every:
        for i in range(1, depth):
            copy = reduce_copy((z + i) % depth, i)
            copy.start()
            sent.append(copy)
    line_part(reduce_copy, True)

    def owned_rows(level):
        return pl.ds(pl.multiple_of(chip * rows + level * owned, owned), owned)

    def gather_copy(i):
        here = whole.at[core, :, owned_rows(z), :]
        return pltpu.make_async_remote_copy(
            src_ref=here,
            dst_ref=here,
            send_sem=lg_sem.at[0, i],
            recv_sem=lg_sem.at[1, z],
            device_id=on_line((z + i) % depth),
            device_id_type=MESH,
        )

    def own():
        for i in range(1, depth):
            other = (z + i) % depth
            arrived(line_recv.at[other], ls_sem.at[1, other])
        local = pl.ds(pl.multiple_of(z * owned, owned), owned)
        limit = widths[core]
        at = chip * rows + z * owned + lax.broadcasted_iota(jnp.int32, (owned, width), 0)
        across = lax.broadcasted_iota(jnp.int32, (owned, width), 1)
        for m in range(3):
            value = part[m, local]
            for i in range(1, depth):
                value += line_recv[(z + i) % depth, m].astype(F32)
            if m == 0:
                pivot = diag_one[core, owned_rows(z)].astype(F32)
                value += jnp.where((at < limit) & (across < limit), pivot, 0.0)
            whole[core, m, owned_rows(z)] = value.astype(BF16)
        for i in range(1, depth):
            gather_copy(i).start()

    def own_end():
        for i in range(1, depth):
            gather_copy(i).wait_send()

    if every:
        own()
    else:
        pl.when(z < owners)(own)

    if every:
        for i in range(1, depth):
            level = (z + i) % depth
            arrived(whole.at[core, :, owned_rows(level), :], lg_sem.at[1, level])
    else:
        for t in range(owners):

            @pl.when(z != t)
            def _():
                arrived(whole.at[core, :, owned_rows(t), :], lg_sem.at[1, t])

    def chip_rows(c, s):
        return whole.at[s, :, pl.ds(pl.multiple_of(c * rows, rows), rows), :]

    here = chip_rows(chip, core)
    for i in range(1, n):
        sent.append(send(here, here, pg_sem.at[0, i], pg_sem.at[1, chip], on_chip((chip + i) % n)))
    sent.append(send(here, here, fg_sem.at[0, chip], fg_sem.at[1, chip], sibling))

    for i in range(1, depth):
        other = (z + i) % depth
        arrived(prod_recv.at[other], p_sem.at[1, other])

    def masked_link(s):
        at = lax.broadcasted_iota(jnp.int32, (width, width), 0)
        across = lax.broadcasted_iota(jnp.int32, (width, width), 1)
        kept = (at < widths[s]) & (across < widths[2 + s])
        return jnp.where(kept, link[s].astype(F32), 0.0).astype(BF16)

    links = [masked_link(s) for s in range(2)]
    totals = []
    for p in range(PIECES):
        value = prod[p, pl.ds(pl.multiple_of(z * share, share), share)]
        for i in range(1, depth):
            value += prod_recv[(z + i) % depth, p].astype(F32)
        totals.append(value)
    for s in range(2):
        new = (-totals[s]).astype(BF16)
        col_one_out[:, s * width : (s + 1) * width] = new
        second = totals[2 + s] + jnp.dot(new, links[s], preferred_element_type=F32)
        col_two_out[:, s * width : (s + 1) * width] = (-(second * member[2 + s])).astype(BF16)

    for i in range(1, n):
        other = (chip + i) % n
        there = chip_rows(other, core)
        arrived(there, pg_sem.at[1, other])
        sent.append(send(there, there, fg_sem.at[0, other], fg_sem.at[1, other], sibling))
    for c in range(n):
        arrived(chip_rows(c, 1 - core), fg_sem.at[1, c])

    for s in range(2):
        block = whole[s, 0]
        cross = whole[s, 1]
        block_one_out[s] = block
        parent = cross.astype(F32).T - jnp.dot(block, links[s], preferred_element_type=F32)
        parent = parent.astype(BF16)
        parent_out[s] = parent
        at = lax.broadcasted_iota(jnp.int32, (width, width), 0)
        across = lax.broadcasted_iota(jnp.int32, (width, width), 1)
        limit = widths[2 + s]
        value = jnp.where((at < limit) & (across < limit), diag_two[s].astype(F32), 0.0)
        value += whole[s, 2].astype(F32)
        value -= jnp.dot(cross, links[s], preferred_element_type=F32)
        value -= left_t(links[s], parent)
        block_two_out[s] = value.astype(BF16)

    for copy in sent + line_copies:
        copy.wait_send()
    line_part(reduce_copy, False)
    if small:
        spread(False)
    else:
        pl.when(jnp.logical_not(is_relay))(first.wait_send)
        pl.when(is_relay)(functools.partial(spread, False))
        pl.when(jnp.logical_not(is_relay))(functools.partial(forward, mine, False))
        for i in range(1, PIECES):
            forward((mine + i) % PIECES, False)
    if every:
        own_end()
    else:
        pl.when(z < owners)(own_end)


def solution(mesh):
    n = mesh.shape["row"] // 2
    depth = mesh.shape["col"]

    def local(inverse, panel_one, anc_one, diag_one, panel_two, link_two, anc_two, diag_two, widths):
        width = diag_one.shape[-1]
        share = panel_one.shape[0]
        rows = width // n
        owners = max(1, min(depth, rows // 16))
        assert inverse.shape == (width, 2 * width) and n == depth and n % PIECES == 0
        assert share * depth == width and panel_one.shape[1] == 2 * width
        chunks = depth if n == PIECES else 1
        vmem = pl.BlockSpec(memory_space=pltpu.VMEM)
        smem = pl.BlockSpec(memory_space=pltpu.SMEM)
        hbm = pl.BlockSpec(memory_space=pl.ANY)
        dma = pltpu.SemaphoreType.DMA
        square = (2, width, width)
        return pl.pallas_call(
            functools.partial(kernel, n, depth),
            out_shape=(
                jax.ShapeDtypeStruct(panel_one.shape, BF16),
                jax.ShapeDtypeStruct(square, BF16),
                jax.ShapeDtypeStruct(panel_two.shape, BF16),
                jax.ShapeDtypeStruct(square, BF16),
                jax.ShapeDtypeStruct(square, BF16),
            ),
            in_specs=[vmem, vmem, smem, smem, smem, hbm, hbm, hbm, hbm],
            out_specs=[vmem] * 5,
            scratch_shapes=[
                pltpu.VMEM(inverse.shape, BF16),
                pltpu.VMEM(square, BF16),
                pltpu.VMEM(square, BF16),
                pltpu.VMEM(square, BF16),
                pltpu.VMEM((depth, PIECES, share, width), BF16),
                pltpu.VMEM((PIECES, share, width), BF16),
                pltpu.VMEM((PIECES, 2, depth, share, width), BF16),
                pltpu.VMEM((PIECES, width, width), F32),
                pltpu.VMEM((depth, PIECES, share, width), BF16),
                pltpu.VMEM((depth, PIECES, share, width), BF16),
                pltpu.VMEM((3, width, width), BF16),
                pltpu.VMEM((3, width, width), BF16),
                pltpu.VMEM((3, width, width), F32),
                pltpu.VMEM((n, 3, rows, width), BF16),
                pltpu.VMEM((n, 3, rows, width), BF16),
                pltpu.VMEM((3, rows, width), F32),
                pltpu.VMEM((owners, 3, rows // owners, width), BF16),
                pltpu.VMEM((depth, 3, rows // owners, width), BF16),
                pltpu.VMEM((2, 3, width, width), BF16),
                dma((4,)),
                dma((2, PIECES)),
                dma((2, max(depth, PIECES))),
                dma((chunks, n)),
                dma((PIECES, chunks)),
                dma((PIECES, chunks)),
                dma((PIECES, chunks)),
                dma((2, depth)),
                dma((2, depth)),
                dma((2,)),
                dma((2, n)),
                dma((2, depth)),
                dma((2, depth)),
                dma((2, n)),
                dma((2, n)),
            ],
            compiler_params=pltpu.CompilerParams(
                collective_id=0, has_side_effects=True, vmem_limit_bytes=40 * 1024 * 1024
            ),
            cost_estimate=pl.CostEstimate(flops=10**9, bytes_accessed=3 * 10**6, transcendentals=0),
        )(panel_one, panel_two, anc_one, anc_two, widths, inverse, diag_one, diag_two, link_two)

    in_specs = (
        P("row", "col"),
        P(("row", "col"), None),
        P(),
        P(),
        P(("row", "col"), None),
        P(),
        P(),
        P(),
        P(),
    )
    out_specs = (P(("row", "col"), None), P(), P(("row", "col"), None), P(), P())
    return jax.shard_map(local, mesh=mesh, in_specs=in_specs, out_specs=out_specs, check_vma=False)
```

time: 266 us -> 65.3 us (0.25)
  waiting for transfers between devices: 217 us -> 0 us
  Pallas kernels: 0 us -> 53.5 us
  blocking collectives: 15.3 us -> 0 us
  between operations: 14 us -> 0.66 us
  matrix products: 6.66 us -> 0 us
  local copies, waits for them, and re-layouts: 6.24 us -> 10.8 us
  other arithmetic: 4.32 us -> 0 us
    psum x2 -> x0, waiting for transfers between devices: 190 us -> none  [the longest x1 131 us: local(): diag_total = lax.psum(diag_part, ('row', 'col'))]
    pallas_call x0 -> x1, Pallas kernels: none -> 53.5 us  [local(): pl.pallas_call(functools.partial(kernel, n, depth), out_shape=(jax.ShapeD...]
    unnamed x4 -> x0, waiting for transfers between devices: 27.2 us -> none
    all_gather x1 -> x0, blocking collectives: 15.3 us -> none  [columns_joint(): whole_rows = lax.all_gather(share_block, 'col', axis=0, tiled=True)]
    unnamed x26 -> x23, local copies, waits for them, and re-layouts: 3.89 us -> 10.8 us
    dot_general x7 -> x0, matrix products: 6.66 us -> none  [the longest x1 1.68 us: product_joint(): jnp.dot(ancestor_inverse, lower_columns, preferred_element_type=jnp.float32)]
  transfers between devices with their start and end apart: 3 -> 0, of which waited for: 3 -> 0; matrix products, arithmetic and copies ran while one was open for 1% -> 0% of each run, Pallas kernels for 0% -> 0%
where the time goes in v1:
time: 65.3 us; the launch traced here: 65 us
  Pallas kernels  53.5 us (82%)
  local copies, waits for them, and re-layouts  10.8 us (17%)
  between operations  0.66 us (1%)
    pallas_call x1, Pallas kernels, local(): pl.pallas_call(functools.partial(kernel, n, depth), out_shape=(jax.ShapeD...  53.5 us
    unnamed x23, local copies, waits for them, and re-layouts  10.8 us

profile of v1, /device:TPU:1, one launch (start us, length us, event | category | flops | bytes accessed | tf_op | source)
XLA Modules:
  0.0 65.0 jit_solution(13070387350545772915)
XLA Ops:
  0.6 0.0 copy-start
  0.6 0.9 %copy-done = bf16[256,512]{1,0:T(8,128)(2,1)S(1)} copy-done((bf16[256,512]{1,0:T(8,128)(2,1)S(1)}, bf16[256,512]{1,0:T(8,128)(2,1)}, u32[]{:S(2)}) %copy-start) | copy-done | bytes 262168
  1.6 0.0 copy-start.1
  1.6 0.9 %copy-done.1 = bf16[2,256,256]{2,1,0:T(8,128)(2,1)S(1)} copy-done((bf16[2,256,256]{2,1,0:T(8,128)(2,1)S(1)}, bf16[2,256,256]{2,1,0:T(8,128)(2,1)}, u32[]{:S(2)}) %copy-start.1) | copy-done | bytes 262168
  2.5 0.0 copy-start.2
  2.5 0.9 %copy-done.2 = bf16[2,256,256]{2,1,0:T(8,128)(2,1)S(1)} copy-done((bf16[2,256,256]{2,1,0:T(8,128)(2,1)S(1)}, bf16[2,256,256]{2,1,0:T(8,128)(2,1)}, u32[]{:S(2)}) %copy-start.2) | copy-done | bytes 262168
  3.5 0.0 copy-start.3
  3.5 0.9 %copy-done.3 = bf16[2,256,256]{2,1,0:T(8,128)(2,1)S(1)} copy-done((bf16[2,256,256]{2,1,0:T(8,128)(2,1)S(1)}, bf16[2,256,256]{2,1,0:T(8,128)(2,1)}, u32[]{:S(2)}) %copy-start.3) | copy-done | bytes 262168
  4.4 0.0 copy-start.4
  4.4 0.8 %copy-done.4 = bf16[64,512]{1,0:T(8,128)(2,1)S(1)} copy-done((bf16[64,512]{1,0:T(8,128)(2,1)S(1)}, bf16[64,512]{1,0:T(8,128)(2,1)}, u32[]{:S(2)}) %copy-start.4) | copy-done | bytes 65560
  5.3 0.0 copy-start.5
  5.3 0.8 %copy-done.5 = bf16[64,512]{1,0:T(8,128)(2,1)S(1)} copy-done((bf16[64,512]{1,0:T(8,128)(2,1)S(1)}, bf16[64,512]{1,0:T(8,128)(2,1)}, u32[]{:S(2)}) %copy-start.5) | copy-done | bytes 65560
  6.1 0.0 copy-start.6
  6.1 0.7 %copy-done.6 = s32[2,7]{1,0:T(2,128)S(1)} copy-done((s32[2,7]{1,0:T(2,128)S(1)}, s32[2,7]{1,0:T(2,128)}, u32[]{:S(2)}) %copy-start.6) | copy-done | bytes 80
  6.8 0.0 copy-start.7
  6.8 0.7 %copy-done.7 = s32[2,6]{1,0:T(2,128)S(1)} copy-done((s32[2,6]{1,0:T(2,128)S(1)}, s32[2,6]{1,0:T(2,128)}, u32[]{:S(2)}) %copy-start.7) | copy-done | bytes 72
  7.5 0.0 copy-start.8
  7.5 0.7 %copy-done.8 = s32[4]{0:T(128)S(1)} copy-done((s32[4]{0:T(128)S(1)}, s32[4]{0:T(128)}, u32[]{:S(2)}) %copy-start.8) | copy-done | bytes 40
  8.1 53.5 %shard_map.128 = (bf16[64,512]{1,0:T(8,128)(2,1)S(1)}, bf16[2,256,256]{2,1,0:T(8,128)(2,1)S(1)}, bf16[64,512]{1,0:T(8,128)(2,1)S(1)}, bf16[2,256,256]{2,1,0:T(8,128)(2,1)S(1)}, bf16[2,256,256]{2,1,0:T(8,128)(2,1)S(1)}) custom-call(bf16[64,512]{1,0:T(8,128)(2,1)S(1)} %copy-done.4, bf16[64,512]{1,0:T(8,128)(2,1)S(1)} %copy-done.5, s32[2,7]{1,0:T(2,128)S(1)} %copy-done.6, ...), custom_call_target="tpu_custom_call" | custom-call | flops 1000000000 | bytes 3000000 | tf_op jit(solution)/shard_map/pallas_call | solution.py:477
  61.6 0.6 copy.19
  62.2 0.7 %copy.20 = bf16[2,256,256]{2,1,0:T(8,128)(2,1)} copy(bf16[2,256,256]{2,1,0:T(8,128)(2,1)S(1)} %get-tuple-element.11) | data formatting | bytes 524288
  62.9 0.6 copy.21
  63.6 0.7 %copy.22 = bf16[2,256,256]{2,1,0:T(8,128)(2,1)} copy(bf16[2,256,256]{2,1,0:T(8,128)(2,1)S(1)} %get-tuple-element.13) | data formatting | bytes 524288
  64.3 0.7 %copy.23 = bf16[2,256,256]{2,1,0:T(8,128)(2,1)} copy(bf16[2,256,256]{2,1,0:T(8,128)(2,1)S(1)} %get-tuple-element.14) | data formatting | bytes 524288
Async XLA Ops:
  0.6 1.0 %copy-start = (bf16[256,512]{1,0:T(8,128)(2,1)S(1)}, bf16[256,512]{1,0:T(8,128)(2,1)}, u32[]{:S(2)}) copy-start(bf16[256,512]{1,0:T(8,128)(2,1)} %inv_hbm.1) | copy-start | bytes 786436
  1.6 0.9 %copy-start.1 = (bf16[2,256,256]{2,1,0:T(8,128)(2,1)S(1)}, bf16[2,256,256]{2,1,0:T(8,128)(2,1)}, u32[]{:S(2)}) copy-start(bf16[2,256,256]{2,1,0:T(8,128)(2,1)} %diag_one_hbm.1) | copy-start | bytes 786436
  2.5 0.9 %copy-start.2 = (bf16[2,256,256]{2,1,0:T(8,128)(2,1)S(1)}, bf16[2,256,256]{2,1,0:T(8,128)(2,1)}, u32[]{:S(2)}) copy-start(bf16[2,256,256]{2,1,0:T(8,128)(2,1)} %diag_two_hbm.1) | copy-start | bytes 786436
  3.5 0.9 %copy-start.3 = (bf16[2,256,256]{2,1,0:T(8,128)(2,1)S(1)}, bf16[2,256,256]{2,1,0:T(8,128)(2,1)}, u32[]{:S(2)}) copy-start(bf16[2,256,256]{2,1,0:T(8,128)(2,1)} %link_hbm.1) | copy-start | bytes 786436
  4.4 0.8 %copy-start.4 = (bf16[64,512]{1,0:T(8,128)(2,1)S(1)}, bf16[64,512]{1,0:T(8,128)(2,1)}, u32[]{:S(2)}) copy-start(bf16[64,512]{1,0:T(8,128)(2,1)} %panel_one.1) | copy-start | bytes 196612
  5.3 0.8 %copy-start.5 = (bf16[64,512]{1,0:T(8,128)(2,1)S(1)}, bf16[64,512]{1,0:T(8,128)(2,1)}, u32[]{:S(2)}) copy-start(bf16[64,512]{1,0:T(8,128)(2,1)} %panel_two.1) | copy-start | bytes 196612
  6.1 0.7 %copy-start.6 = (s32[2,7]{1,0:T(2,128)S(1)}, s32[2,7]{1,0:T(2,128)}, u32[]{:S(2)}) copy-start(s32[2,7]{1,0:T(2,128)} %anc_one.1) | copy-start | bytes 172
  6.8 0.7 %copy-start.7 = (s32[2,6]{1,0:T(2,128)S(1)}, s32[2,6]{1,0:T(2,128)}, u32[]{:S(2)}) copy-start(s32[2,6]{1,0:T(2,128)} %anc_two.1) | copy-start | bytes 148
  7.5 0.7 %copy-start.8 = (s32[4]{0:T(128)S(1)}, s32[4]{0:T(128)}, u32[]{:S(2)}) copy-start(s32[4]{0:T(128)} %widths.1) | copy-start | bytes 52

commit v2 on v1

--- a/solution.py
+++ b/solution.py
@@ -17,14 +17,22 @@
     return lax.dot_general(a, b, (((0,), (0,)), ((), ())), preferred_element_type=F32)
 
 
+def hand_over(*refs):
+    copies = [pltpu.make_async_copy(refs[i], refs[5 + i], refs[10].at[i]) for i in range(5)]
+    for copy in copies:
+        copy.start()
+    for copy in copies:
+        copy.wait()
+
+
 def kernel(
     n,
     depth,
-    panel_one,
-    panel_two,
-    anc_one,
-    anc_two,
-    widths,
+    panel_one_hbm,
+    panel_two_hbm,
+    anc_one_hbm,
+    anc_two_hbm,
+    widths_hbm,
     inv_hbm,
     diag_one_hbm,
     diag_two_hbm,
@@ -34,6 +42,11 @@
     col_two_out,
     parent_out,
     block_two_out,
+    panel_one,
+    panel_two,
+    anc_one,
+    anc_two,
+    widths,
     inv,
     diag_one,
     diag_two,
@@ -98,9 +111,18 @@
         pltpu.make_async_copy(dst, dst, rsem).wait()
 
     loads = []
-    for i, (src, dst) in enumerate(
-        ((inv_hbm, inv), (link_hbm, link), (diag_one_hbm, diag_one), (diag_two_hbm, diag_two))
-    ):
+    pairs = (
+        (anc_one_hbm, anc_one),
+        (anc_two_hbm, anc_two),
+        (widths_hbm, widths),
+        (panel_one_hbm, panel_one),
+        (panel_two_hbm, panel_two),
+        (inv_hbm, inv),
+        (link_hbm, link),
+        (diag_one_hbm, diag_one),
+        (diag_two_hbm, diag_two),
+    )
+    for i, (src, dst) in enumerate(pairs):
         loads.append(pltpu.make_async_copy(src, dst, load_sem.at[i]))
         loads[-1].start()
 
@@ -111,6 +133,8 @@
     for i in range(1, depth):
         pl.semaphore_signal(barrier, inc=1, device_id=on_line((z + i) % depth), device_id_type=MESH)
 
+    for copy in loads[:5]:
+        copy.wait()
     columns = lax.broadcasted_iota(jnp.int32, (share, width), 1)
     member = []
     for p in range(PIECES):
@@ -240,7 +264,7 @@
     else:
         for i in range(1, PIECES):
             forward((mine + i) % PIECES, True)
-    for copy in loads:
+    for copy in loads[5:]:
         copy.wait()
     for p in range(PIECES):
         for level in range(depth if small else 1):
@@ -470,11 +494,10 @@
         assert share * depth == width and panel_one.shape[1] == 2 * width
         chunks = depth if n == PIECES else 1
         vmem = pl.BlockSpec(memory_space=pltpu.VMEM)
-        smem = pl.BlockSpec(memory_space=pltpu.SMEM)
         hbm = pl.BlockSpec(memory_space=pl.ANY)
         dma = pltpu.SemaphoreType.DMA
         square = (2, width, width)
-        return pl.pallas_call(
+        results = pl.pallas_call(
             functools.partial(kernel, n, depth),
             out_shape=(
                 jax.ShapeDtypeStruct(panel_one.shape, BF16),
@@ -483,9 +506,14 @@
                 jax.ShapeDtypeStruct(square, BF16),
                 jax.ShapeDtypeStruct(square, BF16),
             ),
-            in_specs=[vmem, vmem, smem, smem, smem, hbm, hbm, hbm, hbm],
+            in_specs=[hbm] * 9,
             out_specs=[vmem] * 5,
             scratch_shapes=[
+                pltpu.VMEM(panel_one.shape, BF16),
+                pltpu.VMEM(panel_two.shape, BF16),
+                pltpu.SMEM(anc_one.shape, jnp.int32),
+                pltpu.SMEM(anc_two.shape, jnp.int32),
+                pltpu.SMEM(widths.shape, jnp.int32),
                 pltpu.VMEM(inverse.shape, BF16),
                 pltpu.VMEM(square, BF16),
                 pltpu.VMEM(square, BF16),
@@ -505,7 +533,7 @@
                 pltpu.VMEM((owners, 3, rows // owners, width), BF16),
                 pltpu.VMEM((depth, 3, rows // owners, width), BF16),
                 pltpu.VMEM((2, 3, width, width), BF16),
-                dma((4,)),
+                dma((9,)),
                 dma((2, PIECES)),
                 dma((2, max(depth, PIECES))),
                 dma((chunks, n)),
@@ -522,10 +550,18 @@
                 dma((2, n)),
             ],
             compiler_params=pltpu.CompilerParams(
-                collective_id=0, has_side_effects=True, vmem_limit_bytes=40 * 1024 * 1024
+                collective_id=0, has_side_effects=True, vmem_limit_bytes=60 * 1024 * 1024
             ),
             cost_estimate=pl.CostEstimate(flops=10**9, bytes_accessed=3 * 10**6, transcendentals=0),
         )(panel_one, panel_two, anc_one, anc_two, widths, inverse, diag_one, diag_two, link_two)
+        return pl.pallas_call(
+            hand_over,
+            out_shape=tuple(jax.ShapeDtypeStruct(r.shape, r.dtype) for r in results),
+            in_specs=[hbm] * 5,
+            out_specs=[hbm] * 5,
+            scratch_shapes=[dma((5,))],
+            compiler_params=pltpu.CompilerParams(vmem_limit_bytes=60 * 1024 * 1024),
+        )(*results)
 
     in_specs = (
         P("row", "col"),

time: 65.3 us -> 83.6 us (1.28)
  Pallas kernels: 53.5 us -> 82.8 us
  local copies, waits for them, and re-layouts: 10.8 us -> 0 us
    pallas_call x0 -> x1, Pallas kernels: none -> 28.9 us  [local(): pl.pallas_call(hand_over, out_shape=tuple((jax.ShapeDtypeStruct(r.shape,...]
    unnamed x23 -> x0, local copies, waits for them, and re-layouts: 10.8 us -> none
where the time goes in v2:
time: 83.6 us; the launch traced here: 83.4 us
  Pallas kernels  82.8 us (99%)
    pallas_call x1, Pallas kernels, local(): pl.pallas_call(functools.partial(kernel, n, depth), out_shape=(jax.ShapeD...  53.8 us
    pallas_call x1, Pallas kernels, local(): pl.pallas_call(hand_over, out_shape=tuple((jax.ShapeDtypeStruct(r.shape,...  28.9 us

profile of v2, /device:TPU:1, one launch (start us, length us, event | category | flops | bytes accessed | tf_op | source)
XLA Modules:
  0.0 83.4 jit_solution(9176119456701033298)
XLA Ops:
  0.6 53.8 %shard_map.128 = (bf16[64,512]{1,0:T(8,128)(2,1)}, bf16[2,256,256]{2,1,0:T(8,128)(2,1)}, bf16[64,512]{1,0:T(8,128)(2,1)}, bf16[2,256,256]{2,1,0:T(8,128)(2,1)}, bf16[2,256,256]{2,1,0:T(8,128)(2,1)}) custom-call(bf16[64,512]{1,0:T(8,128)(2,1)} %panel_one_hbm.1, bf16[64,512]{1,0:T(8,128)(2,1)} %panel_two_hbm.1, s32[2,7]{1,0:T(2,128)} %anc_one_hbm.1, ...), custom_call_target="tpu_custom_call" | custom-call | flops 1000000000 | bytes 3000000 | tf_op jit(solution)/shard_map/pallas_call | solution.py:500
  54.5 28.9 %shard_map.129 = (bf16[64,512]{1,0:T(8,128)(2,1)}, bf16[2,256,256]{2,1,0:T(8,128)(2,1)}, bf16[64,512]{1,0:T(8,128)(2,1)}, bf16[2,256,256]{2,1,0:T(8,128)(2,1)}, bf16[2,256,256]{2,1,0:T(8,128)(2,1)}) custom-call(bf16[64,512]{1,0:T(8,128)(2,1)} %get-tuple-element.10.refs_0_, bf16[2,256,256]{2,1,0:T(8,128)(2,1)} %get-tuple-element.11.refs_1_, ...), custom_call_target="tpu_custom_call" | custom-call | tf_op jit(solution)/shard_map/pallas_call | solution.py:557

commit v3 on v2

--- a/solution.py
+++ b/solution.py
@@ -18,10 +18,15 @@
 
 
 def hand_over(*refs):
-    copies = [pltpu.make_async_copy(refs[i], refs[5 + i], refs[10].at[i]) for i in range(5)]
-    for copy in copies:
+    sources, targets, held, sem = refs[:5], refs[5:10], refs[10:15], refs[15]
+    loads = [pltpu.make_async_copy(sources[i], held[i], sem.at[0, i]) for i in range(5)]
+    stores = [pltpu.make_async_copy(held[i], targets[i], sem.at[1, i]) for i in range(5)]
+    for copy in loads:
         copy.start()
-    for copy in copies:
+    for load, store in zip(loads, stores):
+        load.wait()
+        store.start()
+    for copy in stores:
         copy.wait()
 
 
@@ -275,11 +280,20 @@
         product = jnp.dot(inv[...], stacked, preferred_element_type=F32) * member[p]
         prod[p] = product
         prod_send[:, p] = product.astype(BF16).reshape(depth, share, width)
-    for i in range(1, depth):
-        other = (z + i) % depth
-        sent.append(
-            send(prod_send.at[other], prod_recv.at[z], p_sem.at[0, i], p_sem.at[1, z], on_line(other))
-        )
+    def send_products(half):
+        for i in range(1, depth):
+            other = (z + i) % depth
+            sent.append(
+                send(
+                    prod_send.at[other, 2 * half : 2 * half + 2],
+                    prod_recv.at[z, 2 * half : 2 * half + 2],
+                    p_sem.at[0, half, i],
+                    p_sem.at[1, half, z],
+                    on_line(other),
+                )
+            )
+
+    send_products(0)
     for i in range(1, depth):
         other = (z + i) % depth
         arrived(lines.at[other], l_sem.at[1, other])
@@ -287,139 +301,149 @@
     def square(ref, p):
         return ref[:, p].reshape(depth * share, width)
 
-    def inner(s):
-        first_lower, second_lower = square(lines, s), square(lines, 2 + s)
-        first, second = square(prod_send, s), square(prod_send, 2 + s)
-        return left_t(first_lower, first), left_t(second_lower, first), left_t(second_lower, second)
-
-    for m, value in enumerate(inner(1 - core)):
-        pair_send[m] = value.astype(BF16)
-    pair = send(pair_send, pair_recv, pair_sem.at[0], pair_sem.at[1], sibling)
-    sent.append(pair)
-    for m, value in enumerate(inner(core)):
+    def inner(s, m):
+        lower = square(lines, s if m == 0 else 2 + s)
+        return left_t(lower, square(prod_send, 2 + s if m == 2 else s))
+
+    rows = width // n
+    owners = line_send.shape[1]
+    owned = rows // owners
+    every = owners == depth
+    first_row = pl.multiple_of(chip * rows, rows)
+
+    def pair_start(m):
+        pair_send[m] = inner(1 - core, m).astype(BF16)
+        sent.append(send(pair_send.at[m], pair_recv.at[m], pair_sem.at[0, m], pair_sem.at[1, m], sibling))
+
+    def plane_start(m):
+        value = inner(core, m)
+        arrived(pair_recv.at[m], pair_sem.at[1, m])
+        value += pair_recv[m].astype(F32)
         sums[m] = value
-    pair.wait_recv()
-
-    rows = width // n
-    for m in range(3):
-        value = sums[m] + pair_recv[m].astype(F32)
-        sums[m] = value
-        plane_send[:, m] = value.astype(BF16).reshape(n, rows, width)
-    for i in range(1, n):
-        other = (chip + i) % n
-        sent.append(
-            send(plane_send.at[other], plane_recv.at[chip], ps_sem.at[0, i], ps_sem.at[1, chip], on_chip(other))
-        )
-    first_row = pl.multiple_of(chip * rows, rows)
-    for i in range(1, n):
-        other = (chip + i) % n
-        arrived(plane_recv.at[other], ps_sem.at[1, other])
-    for m in range(3):
-        value = sums[m, pl.ds(first_row, rows)]
+        plane_send[m] = value.astype(BF16).reshape(n, rows, width)
         for i in range(1, n):
-            value += plane_recv[(chip + i) % n, m].astype(F32)
-        part[m] = value
-
-    owners = line_send.shape[0]
-    owned = rows // owners
-    for m in range(3):
-        line_send[:, m] = part[m].astype(BF16).reshape(owners, owned, width)
-    every = owners == depth
-
-    def line_part(copy_at, start):
-        if every:
-            return
-        for t in range(owners):
-            copy = copy_at(t, t)
-
-            @pl.when(z != t)
-            def _():
-                if start:
-                    copy.start()
-                else:
-                    copy.wait_send()
-
-    def reduce_copy(t, i):
+            other = (chip + i) % n
+            sent.append(
+                send(
+                    plane_send.at[m, other],
+                    plane_recv.at[m, chip],
+                    ps_sem.at[0, m, i],
+                    ps_sem.at[1, m, chip],
+                    on_chip(other),
+                )
+            )
+
+    def reduce_copy(m, t, i):
         return pltpu.make_async_remote_copy(
-            src_ref=line_send.at[t],
-            dst_ref=line_recv.at[z],
-            send_sem=ls_sem.at[0, i],
-            recv_sem=ls_sem.at[1, z],
+            src_ref=line_send.at[m, t],
+            dst_ref=line_recv.at[m, z],
+            send_sem=ls_sem.at[0, m, i],
+            recv_sem=ls_sem.at[1, m, z],
             device_id=on_line(t),
             device_id_type=MESH,
         )
 
-    if every:
-        for i in range(1, depth):
-            copy = reduce_copy((z + i) % depth, i)
-            copy.start()
-            sent.append(copy)
-    line_part(reduce_copy, True)
+    def to_owners(m, start):
+        for t in range(owners):
+            copy = reduce_copy(m, t, t)
+            pl.when(z != t)(copy.start if start else copy.wait_send)
+
+    def line_start(m):
+        value = sums[m, pl.ds(first_row, rows)]
+        for i in range(1, n):
+            other = (chip + i) % n
+            arrived(plane_recv.at[m, other], ps_sem.at[1, m, other])
+            value += plane_recv[m, other].astype(F32)
+        part[m] = value
+        line_send[m] = value.astype(BF16).reshape(owners, owned, width)
+        if every:
+            for i in range(1, depth):
+                copy = reduce_copy(m, (z + i) % depth, i)
+                copy.start()
+                sent.append(copy)
+        else:
+            to_owners(m, True)
 
     def owned_rows(level):
         return pl.ds(pl.multiple_of(chip * rows + level * owned, owned), owned)
 
-    def gather_copy(i):
-        here = whole.at[core, :, owned_rows(z), :]
+    def gather_copy(m, i):
+        here = whole.at[core, m, owned_rows(z), :]
         return pltpu.make_async_remote_copy(
             src_ref=here,
             dst_ref=here,
-            send_sem=lg_sem.at[0, i],
-            recv_sem=lg_sem.at[1, z],
+            send_sem=lg_sem.at[0, m, i],
+            recv_sem=lg_sem.at[1, m, z],
             device_id=on_line((z + i) % depth),
             device_id_type=MESH,
         )
 
-    def own():
+    def own(m):
+        value = part[m, pl.ds(pl.multiple_of(z * owned, owned), owned)]
         for i in range(1, depth):
             other = (z + i) % depth
-            arrived(line_recv.at[other], ls_sem.at[1, other])
-        local = pl.ds(pl.multiple_of(z * owned, owned), owned)
-        limit = widths[core]
-        at = chip * rows + z * owned + lax.broadcasted_iota(jnp.int32, (owned, width), 0)
-        across = lax.broadcasted_iota(jnp.int32, (owned, width), 1)
-        for m in range(3):
-            value = part[m, local]
+            arrived(line_recv.at[m, other], ls_sem.at[1, m, other])
+            value += line_recv[m, other].astype(F32)
+        if m == 0:
+            limit = widths[core]
+            at = chip * rows + z * owned + lax.broadcasted_iota(jnp.int32, (owned, width), 0)
+            across = lax.broadcasted_iota(jnp.int32, (owned, width), 1)
+            pivot = diag_one[core, owned_rows(z)].astype(F32)
+            value += jnp.where((at < limit) & (across < limit), pivot, 0.0)
+        whole[core, m, owned_rows(z)] = value.astype(BF16)
+        for i in range(1, depth):
+            gather_copy(m, i).start()
+
+    def own_end(m):
+        for i in range(1, depth):
+            gather_copy(m, i).wait_send()
+
+    def owners_only(f, m):
+        if every:
+            f(m)
+        else:
+            pl.when(z < owners)(functools.partial(f, m))
+
+    def chip_rows(c, s, m):
+        return whole.at[s, m, pl.ds(pl.multiple_of(c * rows, rows), rows), :]
+
+    def back_start(m):
+        if every:
             for i in range(1, depth):
-                value += line_recv[(z + i) % depth, m].astype(F32)
-            if m == 0:
-                pivot = diag_one[core, owned_rows(z)].astype(F32)
-                value += jnp.where((at < limit) & (across < limit), pivot, 0.0)
-            whole[core, m, owned_rows(z)] = value.astype(BF16)
-        for i in range(1, depth):
-            gather_copy(i).start()
-
-    def own_end():
-        for i in range(1, depth):
-            gather_copy(i).wait_send()
-
-    if every:
-        own()
-    else:
-        pl.when(z < owners)(own)
-
-    if every:
-        for i in range(1, depth):
-            level = (z + i) % depth
-            arrived(whole.at[core, :, owned_rows(level), :], lg_sem.at[1, level])
-    else:
-        for t in range(owners):
-
-            @pl.when(z != t)
-            def _():
-                arrived(whole.at[core, :, owned_rows(t), :], lg_sem.at[1, t])
-
-    def chip_rows(c, s):
-        return whole.at[s, :, pl.ds(pl.multiple_of(c * rows, rows), rows), :]
-
-    here = chip_rows(chip, core)
-    for i in range(1, n):
-        sent.append(send(here, here, pg_sem.at[0, i], pg_sem.at[1, chip], on_chip((chip + i) % n)))
-    sent.append(send(here, here, fg_sem.at[0, chip], fg_sem.at[1, chip], sibling))
-
-    for i in range(1, depth):
-        other = (z + i) % depth
-        arrived(prod_recv.at[other], p_sem.at[1, other])
+                level = (z + i) % depth
+                arrived(whole.at[core, m, owned_rows(level), :], lg_sem.at[1, m, level])
+        else:
+            for t in range(owners):
+                there = whole.at[core, m, owned_rows(t), :]
+                pl.when(z != t)(functools.partial(arrived, there, lg_sem.at[1, m, t]))
+        here = chip_rows(chip, core, m)
+        for i in range(1, n):
+            sent.append(send(here, here, pg_sem.at[0, m, i], pg_sem.at[1, m, chip], on_chip((chip + i) % n)))
+        sent.append(send(here, here, fg_sem.at[0, m, chip], fg_sem.at[1, m, chip], sibling))
+
+    def back_forward(m):
+        for i in range(1, n):
+            other = (chip + i) % n
+            there = chip_rows(other, core, m)
+            arrived(there, pg_sem.at[1, m, other])
+            sent.append(send(there, there, fg_sem.at[0, m, other], fg_sem.at[1, m, other], sibling))
+
+    for m in range(3):
+        pair_start(m)
+    for m in range(3):
+        plane_start(m)
+    line_start(0)
+    line_start(1)
+    owners_only(own, 0)
+    line_start(2)
+    owners_only(own, 1)
+    back_start(0)
+    owners_only(own, 2)
+    send_products(1)
+    back_start(1)
+    back_forward(0)
+    back_start(2)
+    back_forward(1)
 
     def masked_link(s):
         at = lax.broadcasted_iota(jnp.int32, (width, width), 0)
@@ -428,25 +452,32 @@
         return jnp.where(kept, link[s].astype(F32), 0.0).astype(BF16)
 
     links = [masked_link(s) for s in range(2)]
-    totals = []
-    for p in range(PIECES):
+
+    def total(p):
         value = prod[p, pl.ds(pl.multiple_of(z * share, share), share)]
         for i in range(1, depth):
             value += prod_recv[(z + i) % depth, p].astype(F32)
-        totals.append(value)
+        return value
+
+    def products_arrived(half):
+        for i in range(1, depth):
+            other = (z + i) % depth
+            arrived(prod_recv.at[other, 2 * half : 2 * half + 2], p_sem.at[1, half, other])
+
+    products_arrived(0)
+    added = []
     for s in range(2):
-        new = (-totals[s]).astype(BF16)
+        new = (-total(s)).astype(BF16)
         col_one_out[:, s * width : (s + 1) * width] = new
-        second = totals[2 + s] + jnp.dot(new, links[s], preferred_element_type=F32)
+        added.append(jnp.dot(new, links[s], preferred_element_type=F32))
+    back_forward(2)
+    products_arrived(1)
+    for s in range(2):
+        second = total(2 + s) + added[s]
         col_two_out[:, s * width : (s + 1) * width] = (-(second * member[2 + s])).astype(BF16)
-
-    for i in range(1, n):
-        other = (chip + i) % n
-        there = chip_rows(other, core)
-        arrived(there, pg_sem.at[1, other])
-        sent.append(send(there, there, fg_sem.at[0, other], fg_sem.at[1, other], sibling))
-    for c in range(n):
-        arrived(chip_rows(c, 1 - core), fg_sem.at[1, c])
+    for m in range(3):
+        for c in range(n):
+            arrived(chip_rows(c, 1 - core, m), fg_sem.at[1, m, c])
 
     for s in range(2):
         block = whole[s, 0]
@@ -466,7 +497,6 @@
 
     for copy in sent + line_copies:
         copy.wait_send()
-    line_part(reduce_copy, False)
     if small:
         spread(False)
     else:
@@ -475,10 +505,10 @@
         pl.when(jnp.logical_not(is_relay))(functools.partial(forward, mine, False))
         for i in range(1, PIECES):
             forward((mine + i) % PIECES, False)
-    if every:
-        own_end()
-    else:
-        pl.when(z < owners)(own_end)
+    for m in range(3):
+        if not every:
+            to_owners(m, False)
+        owners_only(own_end, m)
 
 
 def solution(mesh):
@@ -527,11 +557,11 @@
                 pltpu.VMEM((3, width, width), BF16),
                 pltpu.VMEM((3, width, width), BF16),
                 pltpu.VMEM((3, width, width), F32),
-                pltpu.VMEM((n, 3, rows, width), BF16),
-                pltpu.VMEM((n, 3, rows, width), BF16),
+                pltpu.VMEM((3, n, rows, width), BF16),
+                pltpu.VMEM((3, n, rows, width), BF16),
                 pltpu.VMEM((3, rows, width), F32),
-                pltpu.VMEM((owners, 3, rows // owners, width), BF16),
-                pltpu.VMEM((depth, 3, rows // owners, width), BF16),
+                pltpu.VMEM((3, owners, rows // owners, width), BF16),
+                pltpu.VMEM((3, depth, rows // owners, width), BF16),
                 pltpu.VMEM((2, 3, width, width), BF16),
                 dma((9,)),
                 dma((2, PIECES)),
@@ -541,13 +571,13 @@
                 dma((PIECES, chunks)),
                 dma((PIECES, chunks)),
                 dma((2, depth)),
-                dma((2, depth)),
-                dma((2,)),
-                dma((2, n)),
-                dma((2, depth)),
-                dma((2, depth)),
-                dma((2, n)),
-                dma((2, n)),
+                dma((2, 2, depth)),
+                dma((2, 3)),
+                dma((2, 3, n)),
+                dma((2, 3, depth)),
+                dma((2, 3, depth)),
+                dma((2, 3, n)),
+                dma((2, 3, n)),
             ],
             compiler_params=pltpu.CompilerParams(
                 collective_id=0, has_side_effects=True, vmem_limit_bytes=60 * 1024 * 1024
@@ -559,7 +589,7 @@
             out_shape=tuple(jax.ShapeDtypeStruct(r.shape, r.dtype) for r in results),
             in_specs=[hbm] * 5,
             out_specs=[hbm] * 5,
-            scratch_shapes=[dma((5,))],
+            scratch_shapes=[pltpu.VMEM(r.shape, r.dtype) for r in results] + [dma((2, 5))],
             compiler_params=pltpu.CompilerParams(vmem_limit_bytes=60 * 1024 * 1024),
         )(*results)
 

time: 83.6 us -> 53.6 us (0.64)
  Pallas kernels: 82.8 us -> 52.8 us
    pallas_call x1, Pallas kernels: 28.9 us -> 1.98 us  [local(): pl.pallas_call(hand_over, out_shape=tuple((jax.ShapeDtypeStruct(r.shape,...]
    pallas_call x1, Pallas kernels: 53.8 us -> 50.8 us  [local(): pl.pallas_call(functools.partial(kernel, n, depth), out_shape=(jax.ShapeD...]
where the time goes in v3:
time: 53.6 us; the launch traced here: 53.5 us
  Pallas kernels  52.8 us (99%)
  between operations  0.64 us (1%)
    pallas_call x1, Pallas kernels, local(): pl.pallas_call(functools.partial(kernel, n, depth), out_shape=(jax.ShapeD...  50.8 us
    pallas_call x1, Pallas kernels, local(): pl.pallas_call(hand_over, out_shape=tuple((jax.ShapeDtypeStruct(r.shape,...  1.98 us

profile of v3, /device:TPU:1, one launch (start us, length us, event | category | flops | bytes accessed | tf_op | source)
XLA Modules:
  0.0 53.5 jit_solution(17245268405541552304)
XLA Ops:
  0.6 50.8 %shard_map.128 = (bf16[64,512]{1,0:T(8,128)(2,1)}, bf16[2,256,256]{2,1,0:T(8,128)(2,1)}, bf16[64,512]{1,0:T(8,128)(2,1)}, bf16[2,256,256]{2,1,0:T(8,128)(2,1)}, bf16[2,256,256]{2,1,0:T(8,128)(2,1)}) custom-call(bf16[64,512]{1,0:T(8,128)(2,1)} %panel_one_hbm.1, bf16[64,512]{1,0:T(8,128)(2,1)} %panel_two_hbm.1, s32[2,7]{1,0:T(2,128)} %anc_one_hbm.1, ...), custom_call_target="tpu_custom_call" | custom-call | flops 1000000000 | bytes 3000000 | tf_op jit(solution)/shard_map/pallas_call | solution.py:530
  51.5 2.0 %shard_map.129 = (bf16[64,512]{1,0:T(8,128)(2,1)}, bf16[2,256,256]{2,1,0:T(8,128)(2,1)}, bf16[64,512]{1,0:T(8,128)(2,1)}, bf16[2,256,256]{2,1,0:T(8,128)(2,1)}, bf16[2,256,256]{2,1,0:T(8,128)(2,1)}) custom-call(bf16[64,512]{1,0:T(8,128)(2,1)} %get-tuple-element.10.refs_0_, bf16[2,256,256]{2,1,0:T(8,128)(2,1)} %get-tuple-element.11.refs_1_, ...), custom_call_target="tpu_custom_call" | custom-call | tf_op jit(solution)/shard_map/pallas_call | solution.py:587

commit v4 on v3

--- a/solution.py
+++ b/solution.py
@@ -71,6 +71,7 @@
     line_send,
     line_recv,
     whole,
+    fresh,
     load_sem,
     a_sem,
     b_sem,
@@ -195,7 +196,9 @@
     def share_line():
         for i in range(1, depth):
             line_copies.append(
-                send(lines.at[z], lines.at[z], l_sem.at[0, i], l_sem.at[1, z], on_line((z + i) % depth))
+                send(
+                    lines.at[z, 2:4], lines.at[z, 2:4], l_sem.at[0, i], l_sem.at[1, z], on_line((z + i) % depth)
+                )
             )
 
     chunks = [(z + i) % depth for i in range(depth)] if small else [None]
@@ -230,14 +233,12 @@
                     copy.start()
                 else:
                     copy.wait_send()
-            if start and small and t == 0:
-                share_line()
 
     if small:
         spread(True)
     else:
-        share_line()
         pl.when(is_relay)(functools.partial(spread, True))
+    share_line()
 
     def forward(p, start):
         for t, level in enumerate(chunks):
@@ -275,11 +276,6 @@
         for level in range(depth if small else 1):
             arrived(chunk(p, 1 - core, level if small else None), f_recv.at[p, level])
 
-    for p in range(PIECES):
-        stacked = panels[p].reshape(2 * depth * share, width)
-        product = jnp.dot(inv[...], stacked, preferred_element_type=F32) * member[p]
-        prod[p] = product
-        prod_send[:, p] = product.astype(BF16).reshape(depth, share, width)
     def send_products(half):
         for i in range(1, depth):
             other = (z + i) % depth
@@ -293,17 +289,22 @@
                 )
             )
 
-    send_products(0)
+    for p in range(PIECES):
+        stacked = panels[p].reshape(2 * depth * share, width)
+        product = jnp.dot(inv[...], stacked, preferred_element_type=F32) * member[p]
+        prod[p] = product
+        prod_send[:, p] = product.astype(BF16).reshape(depth, share, width)
+        if p % 2 == 1:
+            send_products(p // 2)
     for i in range(1, depth):
         other = (z + i) % depth
-        arrived(lines.at[other], l_sem.at[1, other])
-
-    def square(ref, p):
-        return ref[:, p].reshape(depth * share, width)
+        arrived(lines.at[other, 2:4], l_sem.at[1, other])
 
     def inner(s, m):
-        lower = square(lines, s if m == 0 else 2 + s)
-        return left_t(lower, square(prod_send, 2 + s if m == 2 else s))
+        if m == 2:
+            lower = lines[:, 2 + s].reshape(depth * share, width)
+            return left_t(lower, prod_send[:, 2 + s].reshape(depth * share, width))
+        return left_t(lines[z, 2 * m + s], fresh[s])
 
     rows = width // n
     owners = line_send.shape[1]
@@ -389,7 +390,7 @@
             at = chip * rows + z * owned + lax.broadcasted_iota(jnp.int32, (owned, width), 0)
             across = lax.broadcasted_iota(jnp.int32, (owned, width), 1)
             pivot = diag_one[core, owned_rows(z)].astype(F32)
-            value += jnp.where((at < limit) & (across < limit), pivot, 0.0)
+            value = jnp.where((at < limit) & (across < limit), pivot, 0.0) - value
         whole[core, m, owned_rows(z)] = value.astype(BF16)
         for i in range(1, depth):
             gather_copy(m, i).start()
@@ -428,31 +429,12 @@
             arrived(there, pg_sem.at[1, m, other])
             sent.append(send(there, there, fg_sem.at[0, m, other], fg_sem.at[1, m, other], sibling))
 
-    for m in range(3):
-        pair_start(m)
-    for m in range(3):
-        plane_start(m)
-    line_start(0)
-    line_start(1)
-    owners_only(own, 0)
-    line_start(2)
-    owners_only(own, 1)
-    back_start(0)
-    owners_only(own, 2)
-    send_products(1)
-    back_start(1)
-    back_forward(0)
-    back_start(2)
-    back_forward(1)
-
     def masked_link(s):
         at = lax.broadcasted_iota(jnp.int32, (width, width), 0)
         across = lax.broadcasted_iota(jnp.int32, (width, width), 1)
         kept = (at < widths[s]) & (across < widths[2 + s])
         return jnp.where(kept, link[s].astype(F32), 0.0).astype(BF16)
 
-    links = [masked_link(s) for s in range(2)]
-
     def total(p):
         value = prod[p, pl.ds(pl.multiple_of(z * share, share), share)]
         for i in range(1, depth):
@@ -464,17 +446,34 @@
             other = (z + i) % depth
             arrived(prod_recv.at[other, 2 * half : 2 * half + 2], p_sem.at[1, half, other])
 
+    pair_start(2)
+    plane_start(2)
+    links = [masked_link(s) for s in range(2)]
     products_arrived(0)
-    added = []
     for s in range(2):
         new = (-total(s)).astype(BF16)
+        fresh[s] = new
         col_one_out[:, s * width : (s + 1) * width] = new
-        added.append(jnp.dot(new, links[s], preferred_element_type=F32))
+    pair_start(0)
+    pair_start(1)
+    line_start(2)
+    plane_start(0)
+    plane_start(1)
+    owners_only(own, 2)
+    line_start(0)
+    line_start(1)
+    back_start(2)
+    owners_only(own, 0)
+    owners_only(own, 1)
     back_forward(2)
+    back_start(0)
+    back_start(1)
     products_arrived(1)
     for s in range(2):
-        second = total(2 + s) + added[s]
+        second = total(2 + s) + jnp.dot(fresh[s], links[s], preferred_element_type=F32)
         col_two_out[:, s * width : (s + 1) * width] = (-(second * member[2 + s])).astype(BF16)
+    back_forward(0)
+    back_forward(1)
     for m in range(3):
         for c in range(n):
             arrived(chip_rows(c, 1 - core, m), fg_sem.at[1, m, c])
@@ -483,7 +482,7 @@
         block = whole[s, 0]
         cross = whole[s, 1]
         block_one_out[s] = block
-        parent = cross.astype(F32).T - jnp.dot(block, links[s], preferred_element_type=F32)
+        parent = -cross.astype(F32).T - jnp.dot(block, links[s], preferred_element_type=F32)
         parent = parent.astype(BF16)
         parent_out[s] = parent
         at = lax.broadcasted_iota(jnp.int32, (width, width), 0)
@@ -491,7 +490,7 @@
         limit = widths[2 + s]
         value = jnp.where((at < limit) & (across < limit), diag_two[s].astype(F32), 0.0)
         value += whole[s, 2].astype(F32)
-        value -= jnp.dot(cross, links[s], preferred_element_type=F32)
+        value += jnp.dot(cross, links[s], preferred_element_type=F32)
         value -= left_t(links[s], parent)
         block_two_out[s] = value.astype(BF16)
 
@@ -563,6 +562,7 @@
                 pltpu.VMEM((3, owners, rows // owners, width), BF16),
                 pltpu.VMEM((3, depth, rows // owners, width), BF16),
                 pltpu.VMEM((2, 3, width, width), BF16),
+                pltpu.VMEM((2, share, width), BF16),
                 dma((9,)),
                 dma((2, PIECES)),
                 dma((2, max(depth, PIECES))),

time: 53.6 us -> 51.9 us (0.968)
  Pallas kernels: 52.8 us -> 51.1 us
    pallas_call x1, Pallas kernels: 50.8 us -> 49.1 us  [local(): pl.pallas_call(functools.partial(kernel, n, depth), out_shape=(jax.ShapeD...]
where the time goes in v4:
time: 51.9 us; the launch traced here: 51.7 us
  Pallas kernels  51.1 us (98%)
  between operations  0.64 us (1%)
    pallas_call x1, Pallas kernels, local(): pl.pallas_call(functools.partial(kernel, n, depth), out_shape=(jax.ShapeD...  49.1 us
    pallas_call x1, Pallas kernels, local(): pl.pallas_call(hand_over, out_shape=tuple((jax.ShapeDtypeStruct(r.shape,...  1.98 us

profile of v4, /device:TPU:1, one launch (start us, length us, event | category | flops | bytes accessed | tf_op | source)
XLA Modules:
  0.0 51.7 jit_solution(7218229652219239537)
XLA Ops:
  0.6 49.1 %shard_map.128 = (bf16[64,512]{1,0:T(8,128)(2,1)}, bf16[2,256,256]{2,1,0:T(8,128)(2,1)}, bf16[64,512]{1,0:T(8,128)(2,1)}, bf16[2,256,256]{2,1,0:T(8,128)(2,1)}, bf16[2,256,256]{2,1,0:T(8,128)(2,1)}) custom-call(bf16[64,512]{1,0:T(8,128)(2,1)} %panel_one_hbm.1, bf16[64,512]{1,0:T(8,128)(2,1)} %panel_two_hbm.1, s32[2,7]{1,0:T(2,128)} %anc_one_hbm.1, ...), custom_call_target="tpu_custom_call" | custom-call | flops 1000000000 | bytes 3000000 | tf_op jit(solution)/shard_map/pallas_call | solution.py:529
  49.8 2.0 %shard_map.129 = (bf16[64,512]{1,0:T(8,128)(2,1)}, bf16[2,256,256]{2,1,0:T(8,128)(2,1)}, bf16[64,512]{1,0:T(8,128)(2,1)}, bf16[2,256,256]{2,1,0:T(8,128)(2,1)}, bf16[2,256,256]{2,1,0:T(8,128)(2,1)}) custom-call(bf16[64,512]{1,0:T(8,128)(2,1)} %get-tuple-element.10.refs_0_, bf16[2,256,256]{2,1,0:T(8,128)(2,1)} %get-tuple-element.11.refs_1_, ...), custom_call_target="tpu_custom_call" | custom-call | tf_op jit(solution)/shard_map/pallas_call | solution.py:587

commit v5 on v4

--- a/solution.py
+++ b/solution.py
@@ -294,8 +294,8 @@
         product = jnp.dot(inv[...], stacked, preferred_element_type=F32) * member[p]
         prod[p] = product
         prod_send[:, p] = product.astype(BF16).reshape(depth, share, width)
-        if p % 2 == 1:
-            send_products(p // 2)
+        if p == 1:
+            send_products(0)
     for i in range(1, depth):
         other = (z + i) % depth
         arrived(lines.at[other, 2:4], l_sem.at[1, other])
@@ -450,6 +450,7 @@
     plane_start(2)
     links = [masked_link(s) for s in range(2)]
     products_arrived(0)
+    send_products(1)
     for s in range(2):
         new = (-total(s)).astype(BF16)
         fresh[s] = new

time: 51.9 us -> 54.4 us (1.048)
  Pallas kernels: 51.1 us -> 53.6 us
    pallas_call x1, Pallas kernels: 49.1 us -> 51.7 us  [local(): pl.pallas_call(functools.partial(kernel, n, depth), out_shape=(jax.ShapeD...]
where the time goes in v5:
time: 54.4 us; the launch traced here: 54.3 us
  Pallas kernels  53.6 us (99%)
  between operations  0.64 us (1%)
    pallas_call x1, Pallas kernels, local(): pl.pallas_call(functools.partial(kernel, n, depth), out_shape=(jax.ShapeD...  51.7 us
    pallas_call x1, Pallas kernels, local(): pl.pallas_call(hand_over, out_shape=tuple((jax.ShapeDtypeStruct(r.shape,...  1.98 us

profile of v5, /device:TPU:1, one launch (start us, length us, event | category | flops | bytes accessed | tf_op | source)
XLA Modules:
  0.0 54.3 jit_solution(6850248212733183200)
XLA Ops:
  0.6 51.7 %shard_map.128 = (bf16[64,512]{1,0:T(8,128)(2,1)}, bf16[2,256,256]{2,1,0:T(8,128)(2,1)}, bf16[64,512]{1,0:T(8,128)(2,1)}, bf16[2,256,256]{2,1,0:T(8,128)(2,1)}, bf16[2,256,256]{2,1,0:T(8,128)(2,1)}) custom-call(bf16[64,512]{1,0:T(8,128)(2,1)} %panel_one_hbm.1, bf16[64,512]{1,0:T(8,128)(2,1)} %panel_two_hbm.1, s32[2,7]{1,0:T(2,128)} %anc_one_hbm.1, ...), custom_call_target="tpu_custom_call" | custom-call | flops 1000000000 | bytes 3000000 | tf_op jit(solution)/shard_map/pallas_call | solution.py:530
  52.3 2.0 %shard_map.129 = (bf16[64,512]{1,0:T(8,128)(2,1)}, bf16[2,256,256]{2,1,0:T(8,128)(2,1)}, bf16[64,512]{1,0:T(8,128)(2,1)}, bf16[2,256,256]{2,1,0:T(8,128)(2,1)}, bf16[2,256,256]{2,1,0:T(8,128)(2,1)}) custom-call(bf16[64,512]{1,0:T(8,128)(2,1)} %get-tuple-element.10.refs_0_, bf16[2,256,256]{2,1,0:T(8,128)(2,1)} %get-tuple-element.11.refs_1_, ...), custom_call_target="tpu_custom_call" | custom-call | tf_op jit(solution)/shard_map/pallas_call | solution.py:588
